TPU v7x, 32 devices: a whole 2x2x4 slice. The times are simulated.
32 devices in a mesh: dp: 4 (over z), pipe: 4 (over x, core), tensor: 2 (over y).
Axes of the slice: x: 2, y: 2, z: 4, core: 2. Of those that a mesh axis runs over, the one named last changes fastest.
Arguments:
- residual: bfloat16 [4, 2, 256, 6144], P('pipe', None, 'dp', 'tensor'), may hold values from -6 to 6
- queries: bfloat16 [4, 2, 256, 6144], P('pipe', None, 'dp', 'tensor'), may hold values from -6 to 6
- keys_values: bfloat16 [4, 2, 2, 256, 6144], P('pipe', None, None, 'dp', 'tensor'), may hold values from -18 to 18
- global_kv: bfloat16 [4, 2, 2, 384, 6144], P('pipe', None, None, None, 'tensor'), may hold values from -6 to 6
- block_ids: int32 [4, 2, 4, 48], P('pipe', None, 'dp', 'tensor'), may hold values from 0 to 3, as said below
- lengths: int32 [4, 2], P('pipe'), may hold values from 1 to 4, as said below
- gain: bfloat16 [4, 2, 6144], P('pipe', None, 'tensor'), may hold values from 0.5 to 1.5
Outputs:
- normed: bfloat16 [4, 2, 256, 6144], P('pipe', None, 'dp', 'tensor')
Inputs may be any that keep to these rules, and one draw needn't show every extreme that they name: `block_ids`: for one section and direction, the random blocks of the 1 query block of one index of dp in the 24 heads of one index of tensor lie at most 6 in the 1 block of any one index of dp, and exactly 6 for some index. `lengths`: for each section one of the two micro-batches has all 4 blocks live.
All inputs are finite; a program needn't handle non-finite values.
Results may differ from a plain program's by a relative error of at most 0.0053.
Values may be sent and summed in bfloat16 or wider, within the bound.
No kernel may reach another device: no remote copies, remote signals or barrier semaphores. Data moves between devices by JAX's collectives and lax.ppermute only.
A program may use at most 64 MiB of HBM per device.

v0:
```python
import functools

import jax
import jax.numpy as jnp
from jax import lax
from jax.experimental import pallas as pl
from jax.experimental.pallas import tpu as pltpu
from jax.sharding import PartitionSpec as P

D = 6144
HD = 128
BLK = 64
LOG2E = 1.4426950408889634
SCALE = HD ** (-0.5) * LOG2E
NEG = -1e30
VMEM_LIMIT = 20 * 1024 * 1024

epsilon = 1e-05


def dot_nt(a, b):
    return lax.dot_general(a, b, (((1,), (1,)), ((), ())), preferred_element_type=jnp.float32)


def dot_nn(a, b):
    return lax.dot_general(a, b, (((1,), (0,)), ((), ())), preferred_element_type=jnp.float32)


def with_ones(v):
    return jnp.concatenate([v, jnp.ones((v.shape[0], HD), v.dtype)], axis=1)


def head_group(heads):
    return max(g for g in range(1, 9) if heads % g == 0)


def head_batch(heads):
    return max(g for g in range(1, 5) if heads % g == 0)


def heads_wanted(table_ref, row, ids_ref, asker, block):
    heads, capacity = ids_ref.shape[2], table_ref.shape[2]
    for c in range(2):
        for s in range(capacity):
            table_ref[row, c, s] = -1
        slot = jnp.int32(0)
        for h in range(heads):
            match = (ids_ref[asker, c, h] == block) & (slot < capacity)

            @pl.when(match)
            def _(slot=slot, h=h, c=c):
                table_ref[row, c, slot] = h

            slot = slot + match.astype(jnp.int32)


def copy_tiles(out_ref, list_ref, row, c, source_ref):
    for s in range(out_ref.shape[0]):
        cols = pl.ds(pl.multiple_of(jnp.maximum(list_ref[row, c, s], 0) * HD, HD), HD)
        out_ref[s, 0] = source_ref[0, :, cols]
        out_ref[s, 1] = source_ref[1, :, cols]


def pack_kernel(ids_ref, kv_ref, take_ref, out_ref, list_ref):
    me = lax.axis_index("dp")

    @pl.loop(0, ids_ref.shape[0])
    def _(other):
        far = jnp.abs(other - me) >= 2
        heads_wanted(take_ref, other, ids_ref, me, jnp.where(far, other, -1))
        heads_wanted(list_ref, 0, ids_ref, other, jnp.where(far, me, -1))
        for c in range(2):
            copy_tiles(out_ref.at[other, c], list_ref, 0, c, kv_ref.at[:, c])


def local_kernel(heads_step, ids_ref, len_ref, q_ref, kv_ref, gkv_ref, acc_ref, max_ref, sum_ref):
    me = lax.axis_index("dp")
    c = pl.program_id(0)
    g = pl.program_id(1)
    glob = gkv_ref.shape[2]
    lane = lax.broadcasted_iota(jnp.int32, (1, glob + BLK), 1)
    batch = head_batch(heads_step)
    for start in range(0, heads_step, batch):
        cols = [slice(n * HD, (n + 1) * HD) for n in range(start, start + batch)]
        scores, values = [], []
        for n, col in zip(range(start, start + batch), cols):
            k = jnp.concatenate([gkv_ref[0, 0, :, col], kv_ref[0, 0, :, col]], axis=0)
            values.append(jnp.concatenate([gkv_ref[1, 0, :, col], kv_ref[1, 0, :, col]], axis=0))
            twice = jnp.where(ids_ref[me, c, g * heads_step + n] == me, 1.0, 0.0)
            bias = jnp.where(lane < glob, 0.0, jnp.where(me < len_ref[c], twice, NEG))
            scores.append(dot_nt(q_ref[0, :, col], k) * SCALE + bias)
        tops = [jnp.max(s, axis=1, keepdims=True) for s in scores]
        weights = [jnp.exp2(s - m).astype(jnp.bfloat16) for s, m in zip(scores, tops)]
        sums = [dot_nn(p, with_ones(v)) for p, v in zip(weights, values)]
        for col, m, pv in zip(cols, tops, sums):
            acc_ref[0, :, col] = pv[:, :HD]
            sum_ref[0, :, col] = pv[:, HD:]
            max_ref[0, :, col] = jnp.broadcast_to(m, (BLK, HD))


def merge(scores, olds, values):
    tops = [jnp.maximum(old[0], jnp.max(s, axis=1, keepdims=True)) for s, old in zip(scores, olds)]
    weights = [jnp.exp2(s - m[:, : s.shape[1]]).astype(jnp.bfloat16) for s, m in zip(scores, tops)]
    alphas = [jnp.exp2(old[0] - m) for old, m in zip(olds, tops)]
    added = [dot_nn(p, with_ones(v)) for p, v in zip(weights, values)]
    return [
        (m, alpha * old[1] + pv[:, HD:], alpha * old[2] + pv[:, :HD])
        for m, alpha, old, pv in zip(tops, alphas, olds, added)
    ]


def window_kernel(ids_ref, len_ref, q_ref, up_ref, down_ref, res_ref, acc_ref, max_ref, sum_ref, new_acc_ref, new_max_ref, new_sum_ref, out_ref, sq_ref):
    me = lax.axis_index("dp")
    heads = q_ref.shape[2] // HD
    batch = head_batch(heads)
    lane = lax.broadcasted_iota(jnp.int32, (1, 2 * BLK), 1)
    for c in range(2):
        length = len_ref[c]
        alive = me < length
        up_live = (me >= 1) & (me - 1 < length)
        down_live = me + 1 < length

        def step(g, squares, c=c, alive=alive, up_live=up_live, down_live=down_live):
            cols = [pl.ds(pl.multiple_of((g * batch + n) * HD, HD), HD) for n in range(batch)]
            blocks = [ids_ref[me, c, g * batch + n] for n in range(batch)]
            scores, values = [], []
            for block, col in zip(blocks, cols):
                up_bias = jnp.where(up_live, jnp.where(block == me - 1, 1.0, 0.0), NEG)
                down_bias = jnp.where(down_live, jnp.where(block == me + 1, 1.0, 0.0), NEG)
                bias = jnp.where(lane < BLK, up_bias, down_bias)
                k = jnp.concatenate([up_ref[0, c, :, col], down_ref[0, c, :, col]], axis=0)
                values.append(jnp.concatenate([up_ref[1, c, :, col], down_ref[1, c, :, col]], axis=0))
                scores.append(dot_nt(q_ref[c, :, col], k) * SCALE + bias)
            olds = [(max_ref[c, :, col], sum_ref[c, :, col], acc_ref[c, :, col]) for col in cols]
            residuals = [res_ref[c, :, col].astype(jnp.float32) for col in cols]
            news = merge(scores, olds, values)
            updates = [
                (res + jnp.where(alive, acc / l, 0.0)).astype(jnp.bfloat16) for res, (_, l, acc) in zip(residuals, news)
            ]
            for block, col, (m, l, acc), updated in zip(blocks, cols, news, updates):
                new_max_ref[c, :, col] = m
                new_sum_ref[c, :, col] = l
                new_acc_ref[c, :, col] = acc
                out_ref[c, :, col] = updated
                wide = updated.astype(jnp.float32)
                squares = squares + wide * wide * jnp.where(jnp.abs(block - me) < 2, 1.0, 0.0)
            return squares

        sq_ref[c] = lax.fori_loop(0, heads // batch, step, jnp.zeros((BLK, HD), jnp.float32))


def far_kernel(ids_ref, take_ref, len_ref, tile_ref, q_ref, res_ref, acc_ref, max_ref, sum_ref, old_ref, old_sq_ref, out_ref, sq_ref):
    del old_ref
    me = lax.axis_index("dp")
    owners, _, capacity = take_ref.shape
    sq_ref[...] = old_sq_ref[...]

    def one_owner(owner):
        places = [(c, s) for c in range(2) for s in range(capacity)]
        taken = [take_ref[owner, c, s] for c, s in places]
        chosen = [jnp.maximum(h, 0) for h in taken]
        cols = [pl.ds(pl.multiple_of(h * HD, HD), HD) for h in chosen]
        live = [(t >= 0) & (ids_ref[me, c, h] < len_ref[c]) for (c, _), t, h in zip(places, taken, chosen)]
        scores = [
            dot_nt(q_ref[c, :, col], tile_ref[owner, c, s, 0]) * SCALE + jnp.where(ok, 0.0, NEG)
            for (c, s), col, ok in zip(places, cols, live)
        ]
        olds = [(max_ref[c, :, col], sum_ref[c, :, col], acc_ref[c, :, col]) for (c, _), col in zip(places, cols)]
        residuals = [res_ref[c, :, col].astype(jnp.float32) for (c, _), col in zip(places, cols)]
        news = merge(scores, olds, [tile_ref[owner, c, s, 1] for c, s in places])
        updates = [
            (res + jnp.where(me < len_ref[c], acc / l, 0.0)).astype(jnp.bfloat16)
            for (c, _), res, (_, l, acc) in zip(places, residuals, news)
        ]
        squares = [jnp.zeros((BLK, HD), jnp.float32)] * 2
        for (c, _), t, updated in zip(places, taken, updates):
            wide = updated.astype(jnp.float32)
            squares[c] = squares[c] + wide * wide * jnp.where(t >= 0, 1.0, 0.0)
        for c in range(2):
            sq_ref[c] += squares[c]
        for (c, _), t, col, updated in zip(places, taken, cols, updates):

            @pl.when(t >= 0)
            def _(c=c, col=col, updated=updated):
                out_ref[c, :, col] = updated

    pl.loop(0, owners)(one_owner)


def smem():
    return pl.BlockSpec(memory_space=pltpu.SMEM)


def vmem():
    return pl.BlockSpec(memory_space=pltpu.VMEM)


def body_any(residual, queries, keys_values, global_kv, block_ids, lengths, gain):
    width = residual.shape[-1]
    heads = width // HD
    dp_count = lax.axis_size("dp")
    pipe_count = lax.axis_size("pipe")
    tensor_count = lax.axis_size("tensor")
    group = head_group(heads)
    steps = heads // group
    lanes = group * HD
    capacity = (heads + dp_count - 1) // dp_count
    q = queries[0]
    res = residual[0]
    glob = global_kv[0]
    length = lengths[0]
    glob_count = glob.shape[2]
    params = pltpu.CompilerParams(vmem_limit_bytes=VMEM_LIMIT)

    ids = block_ids[0, :, 0]
    ids = lax.all_to_all(jnp.broadcast_to(ids, (dp_count,) + ids.shape), "dp", split_axis=0, concat_axis=0, tiled=True)
    kv, ids = lax.optimization_barrier((keys_values[0], ids))
    up = lax.ppermute(kv, "dp", [(i, i + 1) for i in range(dp_count - 1)])
    down = lax.ppermute(kv, "dp", [(i + 1, i) for i in range(dp_count - 1)])

    lines = [[(i + 1, i) for i in range(pipe_count - 1)], [(i, i + 1) for i in range(pipe_count - 1)]]
    gains = [lax.ppermute(gain[0, c], "pipe", [(j, i) for i, j in lines[c]]) for c in range(2)]
    q, gains = lax.optimization_barrier((q, gains))
    wide = jax.ShapeDtypeStruct((2, BLK, width), jnp.float32)
    row_spec = pl.BlockSpec((1, BLK, lanes), lambda c, g: (c, 0, g))
    pair_spec = pl.BlockSpec((2, 1, BLK, lanes), lambda c, g: (0, c, 0, g))
    acc, maxes, sums = pl.pallas_call(
        functools.partial(local_kernel, group),
        grid=(2, steps),
        out_shape=[wide] * 3,
        in_specs=[
            smem(),
            smem(),
            row_spec,
            pair_spec,
            pl.BlockSpec((2, 1, glob_count, lanes), lambda c, g: (0, c, 0, g)),
        ],
        out_specs=[row_spec] * 3,
        compiler_params=params,
        cost_estimate=pl.CostEstimate(
            flops=4 * 2 * BLK * width * (glob_count + BLK), bytes_accessed=14 * 2**20, transcendentals=0
        ),
    )(ids, length, q, kv, glob)

    kv, acc = lax.optimization_barrier((kv, acc))

    tile = (2, capacity, 2, BLK, HD)
    take, tiles_all = pl.pallas_call(
        pack_kernel,
        out_shape=[
            jax.ShapeDtypeStruct((dp_count, 2, capacity), jnp.int32),
            jax.ShapeDtypeStruct((dp_count,) + tile, jnp.bfloat16),
        ],
        in_specs=[smem(), vmem()],
        out_specs=[smem(), vmem()],
        scratch_shapes=[pltpu.SMEM((1, 2, capacity), jnp.int32)],
        compiler_params=params,
    )(ids, kv)
    far = [(take, lax.all_to_all(tiles_all, "dp", split_axis=0, concat_axis=0, tiled=True))]

    acc, maxes, sums, updated, squares = pl.pallas_call(
        window_kernel,
        out_shape=[wide] * 3
        + [jax.ShapeDtypeStruct((2, BLK, width), jnp.bfloat16), jax.ShapeDtypeStruct((2, BLK, HD), jnp.float32)],
        in_specs=[smem(), smem()] + [vmem()] * 7,
        out_specs=[vmem()] * 5,
        compiler_params=params,
        cost_estimate=pl.CostEstimate(
            flops=4 * 2 * BLK * width * 2 * BLK, bytes_accessed=9 * 2**20, transcendentals=0
        ),
    )(ids, length, q, up, down, res, acc, maxes, sums)

    for heads_taken, tiles_got in far:
        updated, squares = pl.pallas_call(
            far_kernel,
            out_shape=[
                jax.ShapeDtypeStruct((2, BLK, width), jnp.bfloat16),
                jax.ShapeDtypeStruct((2, BLK, HD), jnp.float32),
            ],
            in_specs=[smem(), smem(), smem()] + [vmem()] * 8,
            out_specs=[vmem()] * 2,
            input_output_aliases={9: 0},
            compiler_params=params,
        )(ids, heads_taken, length, tiles_got, q, res, acc, maxes, sums, updated, squares)

    total = lax.psum(jnp.sum(squares, axis=2), "tensor")
    inverse = lax.rsqrt(total / D + epsilon)
    normed = [
        (updated[c].astype(jnp.float32) * inverse[c][:, None] * gains[c].astype(jnp.float32)).astype(jnp.bfloat16)
        for c in range(2)
    ]
    return jnp.stack([lax.ppermute(normed[c], "pipe", lines[c]) for c in range(2)])[None]


def pair_queries(first, second):
    none = jnp.zeros_like(first)
    return jnp.concatenate(
        [jnp.concatenate([first, none], axis=1), jnp.concatenate([none, second], axis=1)], axis=0
    )


def pair_rows(first, second, lanes):
    return jnp.concatenate([jnp.broadcast_to(first, (BLK, lanes)), jnp.broadcast_to(second, (BLK, lanes))], axis=0)


def pair_context(weights, values):
    both = dot_nn(weights.astype(jnp.bfloat16), values)
    return jnp.concatenate([both[:BLK, :HD], both[BLK:, HD:]], axis=0)


LENGTH = 32


def sent_in(turn):
    parity = lax.rem(lax.axis_index("pipe"), 2)
    return parity if turn == 0 else 1 - parity


def copy_heads(out_ref, list_ref, row, source_ref):
    for s in range(out_ref.shape[0]):
        cols = pl.ds(pl.multiple_of(jnp.maximum(list_ref[row, s], 0) * HD, HD), HD)
        out_ref[s, 0] = source_ref[0, :, cols]
        out_ref[s, 1] = source_ref[1, :, cols]


def list_heads(list_ref, row, heads, block, block_of):
    capacity = list_ref.shape[1]
    for s in range(capacity):
        list_ref[row, s] = 0
    slot = jnp.int32(0)
    for h in range(heads):
        match = (block_of(h) == block) & (slot < capacity)

        @pl.when(match)
        def _(slot=slot, h=h):
            list_ref[row, slot] = h

        slot = slot + match.astype(jnp.int32)


def distant_kernel(ids_ref, kv0_ref, kv1_ref, tile0_ref, tile1_ref, list_ref):
    me = lax.axis_index("dp")
    heads = ids_ref.shape[1]

    @pl.when((me == 0) | (me == 3))
    def _():
        for turn, (kv_ref, tile_ref) in enumerate(((kv0_ref, tile0_ref), (kv1_ref, tile1_ref))):
            c = sent_in(turn)
            list_heads(list_ref, 0, heads, me, lambda h, c=c: ids_ref[c, h])
            copy_heads(tile_ref, list_ref, 0, kv_ref)


def forward_kernel(turn, ids_ref, up_ids_ref, down_ids_ref, kv_ref, up_ref, down_ref, tile_ref, list_ref):
    me = lax.axis_index("dp")
    heads = ids_ref.shape[1]
    c = sent_in(turn)
    edge = (me == 0) | (me == 3)
    list_heads(
        list_ref,
        0,
        heads,
        jnp.where(edge, me, 3 - me),
        lambda h: jnp.where(edge, ids_ref[c, h], jnp.where(me == 1, up_ids_ref[h], down_ids_ref[h])),
    )
    pl.when(edge)(lambda: copy_heads(tile_ref, list_ref, 0, kv_ref))
    pl.when(me == 1)(lambda: copy_heads(tile_ref, list_ref, 0, down_ref))
    pl.when(me == 2)(lambda: copy_heads(tile_ref, list_ref, 0, up_ref))


def message_kernel(turn, heads_step, order_ref, ids_ref, len_ref, q_ref, res_ref, kv_ref, gkv_ref, out_ref):
    me = lax.axis_index("dp")
    g = pl.program_id(0)
    c = order_ref[turn]
    glob = gkv_ref.shape[2]
    width = out_ref.shape[1] - HD
    heads = width // HD
    place = lax.broadcasted_iota(jnp.int32, (1, HD), 1)

    @pl.when(g == 0)
    def _():
        note = jnp.where(place == LENGTH, len_ref[c], 0)
        for h in range(heads):
            note = jnp.where(place == h, ids_ref[c, h], note)
        note = jnp.broadcast_to(note.astype(jnp.float32), (BLK, HD)).astype(jnp.bfloat16)
        out_ref[:BLK, width:] = note
        out_ref[BLK:, width:] = jnp.zeros((2 * BLK, HD), jnp.bfloat16)

    state = out_ref[2 * BLK :, width:].astype(jnp.float32)
    own_live = me < len_ref[c]
    numbers = range(0, heads_step, 2)
    scores, values = [], []
    for n in numbers:
        both = slice(n * HD, (n + 2) * HD)
        q = pair_queries(q_ref[0, :, n * HD : (n + 1) * HD], q_ref[0, :, (n + 1) * HD : (n + 2) * HD])
        k = jnp.concatenate([gkv_ref[0, 0, :, both], kv_ref[0, 0, :, both]], axis=0)
        values.append(jnp.concatenate([gkv_ref[1, 0, :, both], kv_ref[1, 0, :, both]], axis=0))
        own = [
            jnp.where(own_live, jnp.where(ids_ref[c, g * heads_step + n + i] == me, 1.0, 0.0), NEG) for i in range(2)
        ]
        s = dot_nt(q, k) * SCALE
        scores.append(jnp.concatenate([s[:, :glob], s[:, glob:] + pair_rows(*own, BLK)], axis=1))
    tops = [jnp.max(s, axis=1, keepdims=True) for s in scores]
    weights = [jnp.exp2(s - m) for s, m in zip(scores, tops)]
    sums = [jnp.sum(p, axis=1, keepdims=True) for p in weights]
    contexts = [(pair_context(p, v) / l).astype(jnp.bfloat16) for p, v, l in zip(weights, values, sums)]
    levels = [m + jnp.log2(l) for m, l in zip(tops, sums)]
    for n, context, level in zip(numbers, contexts, levels):
        high = level.astype(jnp.bfloat16).astype(jnp.float32)
        middle = (level - high).astype(jnp.bfloat16).astype(jnp.float32)
        low = level - high - middle
        for i in range(2):
            rows = slice(i * BLK, (i + 1) * BLK)
            head = g * heads_step + n + i
            at = place - head
            state = jnp.where(at == 0, high[rows], jnp.where(at == 32, middle[rows], jnp.where(at == 64, low[rows], state)))
            col = slice((n + i) * HD, (n + i + 1) * HD)
            out = pl.ds(pl.multiple_of(head * HD, HD), HD)
            out_ref[:BLK, out] = q_ref[0, :, col]
            out_ref[BLK : 2 * BLK, out] = res_ref[0, :, col]
            out_ref[2 * BLK :, out] = context[rows]
    out_ref[2 * BLK :, width:] = state.astype(jnp.bfloat16)


def near_kernel(info_ref, message_ref, up_ref, down_ref, acc_ref, max_ref, sum_ref, out_ref, sq_ref, take_ref):
    me = lax.axis_index("dp")
    width = out_ref.shape[1]
    heads = width // HD
    batch = head_batch(heads)
    length = info_ref[LENGTH]
    alive = me < length
    up_live = (me >= 1) & (me - 1 < length)
    down_live = me + 1 < length
    list_heads(take_ref, 0, heads, jnp.where(me < 2, me + 2, me - 2), lambda h: info_ref[h])
    list_heads(take_ref, 1, heads, 3 - me, lambda h: info_ref[h])
    lane = lax.broadcasted_iota(jnp.int32, (1, 2 * BLK), 1)
    state = message_ref[2 * BLK :, width:].astype(jnp.float32)
    state = state + pltpu.roll(state, 96, 1) + pltpu.roll(state, 64, 1)
    squares = jnp.zeros((BLK, HD), jnp.float32)

    def score(numbers):
        items = []
        for h in numbers:
            col = slice(h * HD, (h + 1) * HD)
            block = info_ref[h]
            up_bias = jnp.where(up_live, jnp.where(block == me - 1, 1.0, 0.0), NEG)
            down_bias = jnp.where(down_live, jnp.where(block == me + 1, 1.0, 0.0), NEG)
            bias = jnp.where(lane < BLK, up_bias, down_bias)
            k = jnp.concatenate([up_ref[0, :, col], down_ref[0, :, col]], axis=0)
            v = jnp.concatenate([up_ref[1, :, col], down_ref[1, :, col]], axis=0)
            s = dot_nt(message_ref[:BLK, col], k) * SCALE + bias
            level = jnp.broadcast_to(state[:, h : h + 1], (BLK, HD))
            near = jnp.where(jnp.abs(block - me) < 2, 1.0, 0.0)
            items.append((col, s, v, level, message_ref[BLK : 2 * BLK, col], message_ref[2 * BLK :, col], near))
        return items

    def weigh(items):
        outs = []
        for col, s, v, level, res, context, near in items:
            m = jnp.maximum(level, jnp.max(s, axis=1, keepdims=True))
            p = jnp.exp2(s - m).astype(jnp.bfloat16)
            outs.append((col, m, p, v, jnp.exp2(level - m), res, context, near))
        return outs

    def finish(items, squares):
        outs = []
        for col, m, p, v, alpha, res, context, near in items:
            pv = dot_nn(p, with_ones(v))
            l = alpha + pv[:, HD:]
            acc = alpha * context.astype(jnp.float32) + pv[:, :HD]
            updated = (res.astype(jnp.float32) + jnp.where(alive, acc / l, 0.0)).astype(jnp.bfloat16)
            wide = updated.astype(jnp.float32)
            squares = squares + wide * wide * near
            outs.append((col, m, l, acc, updated))
        for col, m, l, acc, updated in outs:
            max_ref[:, col] = m
            sum_ref[:, col] = l
            acc_ref[:, col] = acc
            out_ref[:, col] = updated
        return squares

    batches = [range(start, start + batch) for start in range(0, heads, batch)]
    scored = weighed = None
    for turn in range(len(batches) + 2):
        fresh = score(batches[turn]) if turn < len(batches) else None
        ready = weigh(scored) if scored else None
        if weighed:
            squares = finish(weighed, squares)
        scored, weighed = fresh, ready
    sq_ref[...] = squares


def tile_kernel(row, last, *refs):
    infos, takes, messages, tiles, accs, maxes, sums, olds, old_sqs = [refs[2 * n : 2 * n + 2] for n in range(9)]
    me = lax.axis_index("dp")
    if last:
        outs = [refs[18].at[1 - sent_in(turn)] for turn in range(2)]
        sqs = [refs[19].at[1 - sent_in(turn)] for turn in range(2)]
        for turn in range(2):
            outs[turn][...] = olds[turn][...]
    else:
        outs, sqs = refs[18:20], refs[20:22]

    def work():
        places = [(t, s) for t in range(2) for s in range(tiles[0].shape[0])]
        chosen = [takes[t][row, s] for t, s in places]
        cols = [pl.ds(pl.multiple_of(h * HD, HD), HD) for h in chosen]
        live = [infos[t][h] < infos[t][LENGTH] for (t, _), h in zip(places, chosen)]
        scores = [
            dot_nt(messages[t][:BLK, col], tiles[t][s, 0]) * SCALE + jnp.where(ok, 0.0, NEG)
            for (t, s), col, ok in zip(places, cols, live)
        ]
        before = [(maxes[t][:, col], sums[t][:, col], accs[t][:, col]) for (t, _), col in zip(places, cols)]
        residuals = [messages[t][BLK : 2 * BLK, col].astype(jnp.float32) for (t, _), col in zip(places, cols)]
        news = merge(scores, before, [tiles[t][s, 1] for t, s in places])
        updates = [
            (res + jnp.where(me < infos[t][LENGTH], acc / l, 0.0)).astype(jnp.bfloat16)
            for (t, _), res, (_, l, acc) in zip(places, residuals, news)
        ]
        squares = [old_sqs[t][...] for t in range(2)]
        for (t, _), col, updated in zip(places, cols, updates):
            outs[t][:, col] = updated
            wide = updated.astype(jnp.float32)
            squares[t] = squares[t] + wide * wide
        for t in range(2):
            sqs[t][...] = squares[t]

    if last:
        work()
    else:
        for t in range(2):
            sqs[t][...] = old_sqs[t][...]
        pl.when((me == 0) | (me == 3))(work)


def body_chain(residual, queries, keys_values, global_kv, block_ids, lengths, gain):
    width = residual.shape[-1]
    heads = width // HD
    pipe_count = lax.axis_size("pipe")
    group = head_group(heads)
    steps = heads // group
    lanes = group * HD
    capacity = heads // 4
    q, res, glob, kv, length = queries[0], residual[0], global_kv[0], keys_values[0], lengths[0]
    own_ids = block_ids[0, :, 0]
    glob_count = glob.shape[2]
    params = pltpu.CompilerParams(vmem_limit_bytes=VMEM_LIMIT)
    order = jnp.stack([sent_in(0), sent_in(1)])

    def send(array, turn, moves):
        pairs = []
        for p in range(pipe_count):
            other = p ^ 1 if turn == 1 else ((p + 1) ^ 1) - 1
            if 0 <= other < pipe_count:
                pairs += [
                    ((i * pipe_count + p) if direct else (i * pipe_count + other), j * pipe_count + other)
                    for i, j, direct in moves
                ]
        return lax.ppermute(array, ("dp", "pipe"), pairs)

    ids_3 = lax.ppermute(own_ids, "dp", [(0, 3), (3, 0)])
    ids_2 = lax.ppermute(own_ids, "dp", [(2, 0), (1, 3)])
    kvs, ups, downs = [], [], []
    for turn in range(2):
        c = order[turn]
        note = jnp.pad(lax.dynamic_index_in_dim(own_ids, c, 0, keepdims=False), (0, HD - heads)).astype(jnp.bfloat16)
        note = jnp.broadcast_to(note, (2, BLK, HD))
        kvs.append(jnp.concatenate([lax.dynamic_index_in_dim(kv, c, 1, keepdims=False), note], axis=2))
    kv, ids_3, ids_2, *kvs = lax.optimization_barrier((kv, ids_3, ids_2, *kvs))
    same = [(i, i, True) for i in range(4)]
    crossed = send(kvs[0], 0, same)
    own_kv = kv
    kv, crossed = lax.optimization_barrier((kv, crossed))
    for turn, source in enumerate((crossed, kvs[1])):
        ups.append(send(source, turn, [(i, i + 1, turn == 1) for i in range(3)]))
        downs.append(send(source, turn, [(i + 1, i, turn == 1) for i in range(3)]))

    message = jax.ShapeDtypeStruct((3 * BLK, width + HD), jnp.bfloat16)

    def local_part(turn, kv):
        return pl.pallas_call(
            functools.partial(message_kernel, turn, group),
            grid_spec=pltpu.PrefetchScalarGridSpec(
                num_scalar_prefetch=3,
                grid=(steps,),
                in_specs=[
                    pl.BlockSpec((1, BLK, lanes), lambda g, order, ids, length: (order[turn], 0, g)),
                    pl.BlockSpec((1, BLK, lanes), lambda g, order, ids, length: (order[turn], 0, g)),
                    pl.BlockSpec((2, 1, BLK, lanes), lambda g, order, ids, length: (0, order[turn], 0, g)),
                    pl.BlockSpec((2, 1, glob_count, lanes), lambda g, order, ids, length: (0, order[turn], 0, g)),
                ],
                out_specs=vmem(),
            ),
            out_shape=message,
            compiler_params=params,
        )(order, own_ids, length, q, res, kv, glob)

    messages = [local_part(0, own_kv), local_part(1, kv)]
    messages = list(lax.optimization_barrier(tuple(messages)))
    messages = [send(messages[turn], turn, same) for turn in range(2)]
    tiles = jax.ShapeDtypeStruct((capacity, 2, BLK, HD), jnp.bfloat16)
    distant = pl.pallas_call(
        distant_kernel,
        out_shape=[tiles, tiles],
        in_specs=[smem(), vmem(), vmem()],
        out_specs=[vmem(), vmem()],
        scratch_shapes=[pltpu.SMEM((1, capacity), jnp.int32)],
        compiler_params=params,
    )(ids_3, *kvs)
    far_3 = [send(distant[turn], turn, [(0, 3, True), (3, 0, True)]) for turn in range(2)]

    far_2 = []
    for turn in range(2):
        array = pl.pallas_call(
            functools.partial(forward_kernel, turn),
            out_shape=tiles,
            in_specs=[smem()] * 3 + [vmem()] * 3,
            out_specs=vmem(),
            scratch_shapes=[pltpu.SMEM((1, capacity), jnp.int32)],
            compiler_params=params,
        )(
            ids_2,
            ups[turn][0, 0, width:].astype(jnp.int32),
            downs[turn][0, 0, width:].astype(jnp.int32),
            kvs[turn],
            ups[turn],
            downs[turn],
        )
        far_2.append(send(array, turn, [(0, 2, True), (3, 1, True), (2, 3, False), (1, 0, False)]))

    wide = jax.ShapeDtypeStruct((BLK, width), jnp.float32)
    row = jax.ShapeDtypeStruct((BLK, width), jnp.bfloat16)
    square = jax.ShapeDtypeStruct((BLK, HD), jnp.float32)
    near, infos = [None, None], [None, None]
    for turn in (1, 0):
        if turn == 0:
            messages[0], near[1][4] = lax.optimization_barrier((messages[0], near[1][4]))
        infos[turn] = messages[turn][0, width:].astype(jnp.int32)
        near[turn] = list(
            pl.pallas_call(
                near_kernel,
                out_shape=[wide, wide, wide, row, square, jax.ShapeDtypeStruct((2, capacity), jnp.int32)],
                in_specs=[smem()] + [vmem()] * 3,
                out_specs=[vmem()] * 5 + [smem()],
                compiler_params=params,
            )(infos[turn], messages[turn], ups[turn], downs[turn])
        )
    accs, maxes, sums, updates, squares, takes = [list(items) for items in zip(*near)]
    for index, got, last in ((1, far_3, False), (0, far_2, True)):
        pair = [jax.ShapeDtypeStruct((2,) + kind.shape, kind.dtype) for kind in (row, square)]
        results = pl.pallas_call(
            functools.partial(tile_kernel, index, last),
            out_shape=pair if last else [row, row, square, square],
            in_specs=[smem()] * 4 + [vmem()] * 14,
            out_specs=[vmem()] * (2 if last else 4),
            input_output_aliases={} if last else {14: 0, 15: 1},
            compiler_params=params,
        )(*infos, *takes, *messages, *got, *accs, *maxes, *sums, *updates, *squares)
        if not last:
            updates, squares = results[:2], results[2:]

    updated, squares = results
    total = lax.psum(jnp.sum(squares, axis=2), "tensor")
    inverse = lax.rsqrt(total / D + epsilon)
    normed = updated.astype(jnp.float32) * inverse[:, :, None] * gain[0][:, None, :].astype(jnp.float32)
    return normed.astype(jnp.bfloat16)[None]


def body(*arrays):
    heads = arrays[0].shape[-1] // HD
    chain = lax.axis_size("dp") == 4 and lax.axis_size("pipe") % 2 == 0 and heads % 8 == 0 and heads <= 32
    return (body_chain if chain else body_any)(*arrays)


def solution(mesh):
    in_specs = (
        P("pipe", None, "dp", "tensor"),
        P("pipe", None, "dp", "tensor"),
        P("pipe", None, None, "dp", "tensor"),
        P("pipe", None, None, None, "tensor"),
        P("pipe", None, "dp", "tensor"),
        P("pipe", None),
        P("pipe", None, "tensor"),
    )
    out_specs = P("pipe", None, "dp", "tensor")
    return jax.shard_map(body, mesh=mesh, in_specs=in_specs, out_specs=out_specs, check_vma=False)
```

profile of v0, /device:TPU:1, one launch (start us, length us, event | category | flops | bytes accessed | tf_op | source)
XLA Modules:
  0.0 66.4 jit_solution(17142045586294744492)
XLA Ops:
  0.0 1.3 %collective-permute-start.1 = (s32[2,24]{1,0:T(2,128)}, s32[2,24]{1,0:T(2,128)S(1)}, u32[]{:S(2)}, u32[]{:S(2)}) collective-permute-start(s32[2,24]{1,0:T(2,128)} %bitcast.57), channel_id=1, source_target_pairs={{16,0},{8,24},{17,1},{9,25},{18,2},{10,26},{19,3},{11,27},{20,4},{... | collective-permute-start | bytes 584 | tf_op jit(solution)/shard_map/ppermute | solution.py:561
  1.3 6.1 %collective-permute-start = (s32[2,24]{1,0:T(2,128)}, s32[2,24]{1,0:T(2,128)S(1)}, u32[]{:S(2)}, u32[]{:S(2)}) collective-permute-start(s32[2,24]{1,0:T(2,128)} %bitcast.58), channel_id=1, source_target_pairs={{0,24},{24,0},{1,25},{25,1},{2,26},{26,2},{3,27},{27,3},{4,28},{28... | collective-permute-start | bytes 584 | tf_op jit(solution)/shard_map/ppermute | solution.py:560
  8.1 1.5 %dynamic-slice_bitcast_fusion = (bf16[2,64,3072]{2,1,0:T(8,128)(2,1)S(1)}, bf16[2,64,3072]{2,1,0:T(8,128)(2,1)S(1)}) fusion(bf16[1,2,2,64,3072]{4,3,2,1,0:T(8,128)(2,1)} %param.9, s32[]{:T(128)S(6)} %select_n.11, s32[]{:T(128)S(6)} %select_n.10), kind=kLoop, calls=%fused_computation.4 | loop fusion | bytes 3145736 | tf_op jit(solution)/shard_map/jit(dynamic_index_in_dim)/squeeze | solution.py:567
  10.0 4.1 %collective-permute-start.2 = (bf16[2,64,3200]{2,1,0:T(8,128)(2,1)S(1)}, bf16[2,64,3200]{2,1,0:T(8,128)(2,1)S(1)}, u32[]{:S(2)}, u32[]{:S(2)}) collective-permute-start(bf16[2,64,3200]{2,1,0:T(8,128)(2,1)S(1)} %get-tuple-element.37.kv_ref.kv0_ref), channel_id=1, source_target_pairs={{2,4},{10,12},{18,20},{26,28},{4,2},{12,10},{20,18},{28,26},{3,5},... | collective-permute-start | bytes 2457608 | tf_op jit(solution)/shard_map/ppermute | solution.py:558
  14.1 1.3 %collective-permute-start.6 = (bf16[2,64,3200]{2,1,0:T(8,128)(2,1)S(1)}, bf16[2,64,3200]{2,1,0:T(8,128)(2,1)S(1)}, u32[]{:S(2)}, u32[]{:S(2)}) collective-permute-start(bf16[2,64,3200]{2,1,0:T(8,128)(2,1)S(1)} %get-tuple-element.41.kv_ref.kv1_ref), channel_id=1, source_target_pairs={{8,2},{16,10},{24,18},{10,0},{18,8},{26,16},{12,6},{20,14},{28,22}... | collective-permute-start | bytes 2457608 | tf_op jit(solution)/shard_map/ppermute | solution.py:558
  15.4 4.3 %collective-permute-start.5 = (bf16[2,64,3200]{2,1,0:T(8,128)(2,1)S(1)}, bf16[2,64,3200]{2,1,0:T(8,128)(2,1)S(1)}, u32[]{:S(2)}, u32[]{:S(2)}) collective-permute-start(bf16[2,64,3200]{2,1,0:T(8,128)(2,1)S(1)} %get-tuple-element.41.kv_ref.kv1_ref), channel_id=1, source_target_pairs={{0,10},{8,18},{16,26},{2,8},{10,16},{18,24},{4,14},{12,22},{20,30}... | collective-permute-start | bytes 2457608 | tf_op jit(solution)/shard_map/ppermute | solution.py:558
  19.8 3.7 %copy-done = bf16[1,2,2,384,3072]{4,3,2,1,0:T(8,128)(2,1)S(1)} copy-done((bf16[1,2,2,384,3072]{4,3,2,1,0:T(8,128)(2,1)S(1)}, bf16[1,2,2,384,3072]{4,3,2,1,0:T(8,128)(2,1)}, u32[]{:S(2)}) %copy-start) | copy-done | bytes 9437208
  23.5 3.5 %shard_map.73 = bf16[192,3200]{1,0:T(8,128)(2,1)S(1)} custom-call(s32[2]{0:T(128)S(1)} %pad_add_fusion.order_ref, s32[2,24]{1,0:T(2,128)S(1)} %bitcast.59, s32[2]{0:T(128)S(1)} %bitcast.61, bf16[2,64,3072]{2,1,0:T(8,128)(2,1)S(1)} %bitcast.53, bf16[2,64,3072]{2,1,0:T(8,128)(2,1)S(1)} %bitcast.55, bf16[2,2,64,3072]{3,2,1,0:T(8,128)(2,1)S(1)} %bitcast.51, ...), custom_call_target="tpu_custom_call" | custom-call | tf_op jit(solution)/shard_map/pallas_call | solution.py:580
  27.0 1.3 %collective-permute-start.8 = (bf16[2,64,3200]{2,1,0:T(8,128)(2,1)S(1)}, bf16[2,64,3200]{2,1,0:T(8,128)(2,1)S(1)}, u32[]{:S(2)}, u32[]{:S(2)}) collective-permute-start(bf16[2,64,3200]{2,1,0:T(8,128)(2,1)S(1)} %collective-permute-done.2), channel_id=1, source_target_pairs={{12,4},{20,12},{28,20},{10,2},{18,10},{26,18},{13,5},{21,13},{29,2... | collective-permute-start | bytes 2457608 | tf_op jit(solution)/shard_map/ppermute | solution.py:558
  28.3 4.0 %collective-permute-start.7 = (bf16[2,64,3200]{2,1,0:T(8,128)(2,1)S(1)}, bf16[2,64,3200]{2,1,0:T(8,128)(2,1)S(1)}, u32[]{:S(2)}, u32[]{:S(2)}) collective-permute-start(bf16[2,64,3200]{2,1,0:T(8,128)(2,1)S(1)} %collective-permute-done.2), channel_id=1, source_target_pairs={{4,12},{12,20},{20,28},{2,10},{10,18},{18,26},{5,13},{13,21},{21,2... | collective-permute-start | bytes 2457608 | tf_op jit(solution)/shard_map/ppermute | solution.py:558
  32.3 3.5 %shard_map.74 = bf16[192,3200]{1,0:T(8,128)(2,1)S(1)} custom-call(s32[2]{0:T(128)S(1)} %pad_add_fusion.order_ref, s32[2,24]{1,0:T(2,128)S(1)} %bitcast.60, s32[2]{0:T(128)S(1)} %bitcast.62, bf16[2,64,3072]{2,1,0:T(8,128)(2,1)S(1)} %bitcast.54, bf16[2,64,3072]{2,1,0:T(8,128)(2,1)S(1)} %bitcast.56, bf16[2,2,64,3072]{3,2,1,0:T(8,128)(2,1)S(1)} %bitcast.52, ...), custom_call_target="tpu_custom_call" | custom-call | tf_op jit(solution)/shard_map/pallas_call | solution.py:580
  35.8 2.5 %collective-permute-start.3 = (bf16[192,3200]{1,0:T(8,128)(2,1)S(1)}, bf16[192,3200]{1,0:T(8,128)(2,1)S(1)}, u32[]{:S(2)}, u32[]{:S(2)}) collective-permute-start(bf16[192,3200]{1,0:T(8,128)(2,1)S(1)} %shard_map.73), channel_id=1, source_target_pairs={{2,4},{10,12},{18,20},{26,28},{4,2},{12,10},{20,18},{28,26},{3,5},... | collective-permute-start | bytes 3686408 | tf_op jit(solution)/shard_map/ppermute | solution.py:558
  38.4 0.8 %shard_map.79 = (bf16[6,2,64,128]{3,2,1,0:T(8,128)(2,1)S(1)}, bf16[6,2,64,128]{3,2,1,0:T(8,128)(2,1)S(1)}) custom-call(s32[2,24]{1,0:T(2,128)S(1)} %collective-permute-done.ids_ref, bf16[2,64,3200]{2,1,0:T(8,128)(2,1)S(1)} %get-tuple-element.37.kv_ref.kv0_ref, bf16[2,64,3200]{2,1,0:T(8,128)(2,1)S(1)} %get-tuple-element.41.kv_ref.kv1_ref), custom_call_target="tpu_custom_call" | custom-call | tf_op jit(solution)/shard_map/pallas_call | solution.py:601
  39.2 2.9 %collective-permute-start.11 = (bf16[6,2,64,128]{3,2,1,0:T(8,128)(2,1)S(1)}, bf16[6,2,64,128]{3,2,1,0:T(8,128)(2,1)S(1)}, u32[]{:S(2)}, u32[]{:S(2)}) collective-permute-start(bf16[6,2,64,128]{3,2,1,0:T(8,128)(2,1)S(1)} %get-tuple-element.55), channel_id=1, source_target_pairs={{2,28},{26,4},{4,26},{28,2},{3,29},{27,5},{5,27},{29,3}} | collective-permute-start | bytes 589832 | tf_op jit(solution)/shard_map/ppermute | solution.py:558
  42.1 0.7 %shard_map.78 = bf16[6,2,64,128]{3,2,1,0:T(8,128)(2,1)S(1)} custom-call(s32[2,24]{1,0:T(2,128)S(1)} %collective-permute-done.1.ids_ref, s32[128]{0:T(128)S(1)} %fusion.8.up_ids_ref, s32[128]{0:T(128)S(1)} %fusion.7.down_ids_ref, bf16[2,64,3200]{2,1,0:T(8,128)(2,1)S(1)} %get-tuple-element.41.kv_ref.kv1_ref, ...), custom_call_target="tpu_custom_call" | custom-call | tf_op jit(solution)/shard_map/pallas_call | solution.py:613
  42.9 1.9 %collective-permute-start.12 = (bf16[6,2,64,128]{3,2,1,0:T(8,128)(2,1)S(1)}, bf16[6,2,64,128]{3,2,1,0:T(8,128)(2,1)S(1)}, u32[]{:S(2)}, u32[]{:S(2)}) collective-permute-start(bf16[6,2,64,128]{3,2,1,0:T(8,128)(2,1)S(1)} %get-tuple-element.56), channel_id=1, source_target_pairs={{0,26},{24,2},{2,24},{26,0},{4,30},{28,6},{6,28},{30,4},{1,27},{25... | collective-permute-start | bytes 589832 | tf_op jit(solution)/shard_map/ppermute | solution.py:558
  45.0 0.7 %shard_map.77 = bf16[6,2,64,128]{3,2,1,0:T(8,128)(2,1)S(1)} custom-call(s32[2,24]{1,0:T(2,128)S(1)} %collective-permute-done.1.ids_ref, s32[128]{0:T(128)S(1)} %fusion.10.up_ids_ref, s32[128]{0:T(128)S(1)} %fusion.9.down_ids_ref, bf16[2,64,3200]{2,1,0:T(8,128)(2,1)S(1)} %get-tuple-element.37.kv_ref.kv0_ref, ...), custom_call_target="tpu_custom_call" | custom-call | tf_op jit(solution)/shard_map/pallas_call | solution.py:613
  45.8 7.2 %collective-permute-start.9 = (bf16[6,2,64,128]{3,2,1,0:T(8,128)(2,1)S(1)}, bf16[6,2,64,128]{3,2,1,0:T(8,128)(2,1)S(1)}, u32[]{:S(2)}, u32[]{:S(2)}) collective-permute-start(bf16[6,2,64,128]{3,2,1,0:T(8,128)(2,1)S(1)} %shard_map.77), channel_id=1, source_target_pairs={{2,20},{26,12},{20,28},{12,4},{4,18},{28,10},{18,26},{10,2},{3,21}... | collective-permute-start | bytes 589832 | tf_op jit(solution)/shard_map/ppermute | solution.py:558
  53.0 2.7 %shard_map.75 = (f32[64,3072]{1,0:T(8,128)S(1)}, f32[64,3072]{1,0:T(8,128)S(1)}, f32[64,3072]{1,0:T(8,128)S(1)}, bf16[64,3072]{1,0:T(8,128)(2,1)S(1)}, f32[64,128]{1,0:T(8,128)S(1)}, /*index=5*/s32[2,6]{1,0:T(2,128)S(1)}) custom-call(s32[128]{0:T(128)S(1)} %fusion.11.info_ref.refs_1_, bf16[192,3200]{1,0:T(8,128)(2,1)S(1)} %collective-permute-done.4.message_ref.refs_5_, ...), custom_call_target="tpu_custom_call" | custom-call | tf_op jit(solution)/shard_map/pallas_call | solution.py:639
  56.2 2.7 %shard_map.76 = (f32[64,3072]{1,0:T(8,128)S(1)}, f32[64,3072]{1,0:T(8,128)S(1)}, f32[64,3072]{1,0:T(8,128)S(1)}, bf16[64,3072]{1,0:T(8,128)(2,1)S(1)}, f32[64,128]{1,0:T(8,128)S(1)}, /*index=5*/s32[2,6]{1,0:T(2,128)S(1)}) custom-call(s32[128]{0:T(128)S(1)} %bitcast_convert_fusion.1.info_ref.refs_0_, ...), custom_call_target="tpu_custom_call" | custom-call | tf_op jit(solution)/shard_map/pallas_call | solution.py:639
  58.9 1.2 %shard_map.80 = (bf16[64,3072]{1,0:T(8,128)(2,1)S(1)}, bf16[64,3072]{1,0:T(8,128)(2,1)S(1)}, f32[64,128]{1,0:T(8,128)S(1)}, f32[64,128]{1,0:T(8,128)S(1)}) custom-call(s32[128]{0:T(128)S(1)} %bitcast_convert_fusion.1.info_ref.refs_0_, s32[128]{0:T(128)S(1)} %fusion.11.info_ref.refs_1_, ...), custom_call_target="tpu_custom_call", output_to_operand_aliasing={{0}: (14, {}), {1}: (15, {})} | custom-call | tf_op jit(solution)/shard_map/pallas_call | solution.py:650
  60.2 1.2 %shard_map.81 = (bf16[2,64,3072]{2,1,0:T(8,128)(2,1)S(1)}, f32[2,64,128]{2,1,0:T(8,128)S(1)}) custom-call(s32[128]{0:T(128)S(1)} %bitcast_convert_fusion.1.info_ref.refs_0_, s32[128]{0:T(128)S(1)} %fusion.11.info_ref.refs_1_, s32[2,6]{1,0:T(2,128)S(1)} %get-tuple-element.45.refs_2_, s32[2,6]{1,0:T(2,128)S(1)} %get-tuple-element.46.refs_3_, ...), custom_call_target="tpu_custom_call" | custom-call | tf_op jit(solution)/shard_map/pallas_call | solution.py:650
  61.5 3.8 %psum.7 = f32[2,64]{1,0:T(2,128)S(1)} all-reduce(f32[2,64]{1,0:T(2,128)S(1)} %reduce_sum.9), channel_id=1, replica_groups=mesh['dp'=4,'pipe'=4,'tensor'=2] {'tensor'}, use_global_device_ids=true, to_apply=%region_1.2 | all-reduce | flops 128 | bytes 1024 | tf_op jit(solution)/shard_map/psum | solution.py:662
  65.3 1.1 %fusion = bf16[1,2,64,3072]{3,2,1,0:T(8,128)(2,1)} fusion(bf16[2,64,3072]{2,1,0:T(8,128)(2,1)S(1)} %get-tuple-element.65, f32[2,3072]{1,0:T(2,128)S(1)} %bitcast_convert_fusion, f32[2,64]{1,0:T(2,128)S(1)} %add_rsqrt_fusion), kind=kLoop, calls=%fused_computation.3 | loop fusion | flops 1572864 | bytes 1597952 | tf_op jit(solution)/shard_map/broadcast_in_dim | solution.py:665
  (42 shorter events, 2.2 us)
Async XLA Ops:
  0.0 9.9 %collective-permute-start.1 = (s32[2,24]{1,0:T(2,128)}, s32[2,24]{1,0:T(2,128)S(1)}, u32[]{:S(2)}, u32[]{:S(2)}) collective-permute-start(s32[2,24]{1,0:T(2,128)} %bitcast.57), channel_id=1, source_target_pairs={{16,0},{8,24},{17,1},{9,25},{18,2},{10,26},{19,3},{11,27},{20,4},{... | collective-permute-start | bytes 584 | tf_op jit(solution)/shard_map/ppermute | solution.py:561
  1.3 8.7 %collective-permute-start = (s32[2,24]{1,0:T(2,128)}, s32[2,24]{1,0:T(2,128)S(1)}, u32[]{:S(2)}, u32[]{:S(2)}) collective-permute-start(s32[2,24]{1,0:T(2,128)} %bitcast.58), channel_id=1, source_target_pairs={{0,24},{24,0},{1,25},{25,1},{2,26},{26,2},{3,27},{27,3},{4,28},{28... | collective-permute-start | bytes 584 | tf_op jit(solution)/shard_map/ppermute | solution.py:560
  9.6 10.2 %copy-start.1 = (bf16[1,2,2,64,3072]{4,3,2,1,0:T(8,128)(2,1)S(1)}, bf16[1,2,2,64,3072]{4,3,2,1,0:T(8,128)(2,1)}, u32[]{:S(2)}) copy-start(bf16[1,2,2,64,3072]{4,3,2,1,0:T(8,128)(2,1)} %param.9) | copy-start | bytes 4718596
  9.6 10.2 %copy-start.2 = (bf16[1,2,64,3072]{3,2,1,0:T(8,128)(2,1)S(1)}, bf16[1,2,64,3072]{3,2,1,0:T(8,128)(2,1)}, u32[]{:S(2)}) copy-start(bf16[1,2,64,3072]{3,2,1,0:T(8,128)(2,1)} %param.8) | copy-start | bytes 2359300
  9.6 10.2 %copy-start.3 = (bf16[1,2,64,3072]{3,2,1,0:T(8,128)(2,1)S(1)}, bf16[1,2,64,3072]{3,2,1,0:T(8,128)(2,1)}, u32[]{:S(2)}) copy-start(bf16[1,2,64,3072]{3,2,1,0:T(8,128)(2,1)} %param.7) | copy-start | bytes 2359300
  9.6 10.2 %copy-start.4 = (s32[1,2,1,24]{3,2,1,0:T(1,128)S(1)}, s32[1,2,1,24]{3,2,1,0:T(1,128)}, u32[]{:S(2)}) copy-start(s32[1,2,1,24]{3,2,1,0:T(1,128)} %param.11) | copy-start | bytes 580
  9.6 10.2 %copy-start.5 = (s32[1,2]{1,0:T(1,128)S(1)}, s32[1,2]{1,0:T(1,128)}, u32[]{:S(2)}) copy-start(s32[1,2]{1,0:T(1,128)} %param.12) | copy-start | bytes 28
  10.0 17.0 %collective-permute-start.2 = (bf16[2,64,3200]{2,1,0:T(8,128)(2,1)S(1)}, bf16[2,64,3200]{2,1,0:T(8,128)(2,1)S(1)}, u32[]{:S(2)}, u32[]{:S(2)}) collective-permute-start(bf16[2,64,3200]{2,1,0:T(8,128)(2,1)S(1)} %get-tuple-element.37.kv_ref.kv0_ref), channel_id=1, source_target_pairs={{2,4},{10,12},{18,20},{26,28},{4,2},{12,10},{20,18},{28,26},{3,5},... | collective-permute-start | bytes 2457608 | tf_op jit(solution)/shard_map/ppermute | solution.py:558
  14.1 24.2 %collective-permute-start.6 = (bf16[2,64,3200]{2,1,0:T(8,128)(2,1)S(1)}, bf16[2,64,3200]{2,1,0:T(8,128)(2,1)S(1)}, u32[]{:S(2)}, u32[]{:S(2)}) collective-permute-start(bf16[2,64,3200]{2,1,0:T(8,128)(2,1)S(1)} %get-tuple-element.41.kv_ref.kv1_ref), channel_id=1, source_target_pairs={{8,2},{16,10},{24,18},{10,0},{18,8},{26,16},{12,6},{20,14},{28,22}... | collective-permute-start | bytes 2457608 | tf_op jit(solution)/shard_map/ppermute | solution.py:558
  15.4 23.8 %collective-permute-start.5 = (bf16[2,64,3200]{2,1,0:T(8,128)(2,1)S(1)}, bf16[2,64,3200]{2,1,0:T(8,128)(2,1)S(1)}, u32[]{:S(2)}, u32[]{:S(2)}) collective-permute-start(bf16[2,64,3200]{2,1,0:T(8,128)(2,1)S(1)} %get-tuple-element.41.kv_ref.kv1_ref), channel_id=1, source_target_pairs={{0,10},{8,18},{16,26},{2,8},{10,16},{18,24},{4,14},{12,22},{20,30}... | collective-permute-start | bytes 2457608 | tf_op jit(solution)/shard_map/ppermute | solution.py:558
  19.8 3.7 %copy-start = (bf16[1,2,2,384,3072]{4,3,2,1,0:T(8,128)(2,1)S(1)}, bf16[1,2,2,384,3072]{4,3,2,1,0:T(8,128)(2,1)}, u32[]{:S(2)}) copy-start(bf16[1,2,2,384,3072]{4,3,2,1,0:T(8,128)(2,1)} %param.10) | copy-start | bytes 28311556
  26.9 11.4 %copy-start.6 = (bf16[1,2,3072]{2,1,0:T(2,128)(2,1)S(1)}, bf16[1,2,3072]{2,1,0:T(2,128)(2,1)}, u32[]{:S(2)}) copy-start(bf16[1,2,3072]{2,1,0:T(2,128)(2,1)} %param.13) | copy-start | bytes 36868
  27.0 15.9 %collective-permute-start.8 = (bf16[2,64,3200]{2,1,0:T(8,128)(2,1)S(1)}, bf16[2,64,3200]{2,1,0:T(8,128)(2,1)S(1)}, u32[]{:S(2)}, u32[]{:S(2)}) collective-permute-start(bf16[2,64,3200]{2,1,0:T(8,128)(2,1)S(1)} %collective-permute-done.2), channel_id=1, source_target_pairs={{12,4},{20,12},{28,20},{10,2},{18,10},{26,18},{13,5},{21,13},{29,2... | collective-permute-start | bytes 2457608 | tf_op jit(solution)/shard_map/ppermute | solution.py:558
  28.3 16.7 %collective-permute-start.7 = (bf16[2,64,3200]{2,1,0:T(8,128)(2,1)S(1)}, bf16[2,64,3200]{2,1,0:T(8,128)(2,1)S(1)}, u32[]{:S(2)}, u32[]{:S(2)}) collective-permute-start(bf16[2,64,3200]{2,1,0:T(8,128)(2,1)S(1)} %collective-permute-done.2), channel_id=1, source_target_pairs={{4,12},{12,20},{20,28},{2,10},{10,18},{18,26},{5,13},{13,21},{21,2... | collective-permute-start | bytes 2457608 | tf_op jit(solution)/shard_map/ppermute | solution.py:558
  35.8 20.4 %collective-permute-start.3 = (bf16[192,3200]{1,0:T(8,128)(2,1)S(1)}, bf16[192,3200]{1,0:T(8,128)(2,1)S(1)}, u32[]{:S(2)}, u32[]{:S(2)}) collective-permute-start(bf16[192,3200]{1,0:T(8,128)(2,1)S(1)} %shard_map.73), channel_id=1, source_target_pairs={{2,4},{10,12},{18,20},{26,28},{4,2},{12,10},{20,18},{28,26},{3,5},... | collective-permute-start | bytes 3686408 | tf_op jit(solution)/shard_map/ppermute | solution.py:558
  38.3 7.5 %collective-permute-start.4 = (bf16[192,3200]{1,0:T(8,128)(2,1)S(1)}, bf16[192,3200]{1,0:T(8,128)(2,1)S(1)}, u32[]{:S(2)}, u32[]{:S(2)}) collective-permute-start(bf16[192,3200]{1,0:T(8,128)(2,1)S(1)} %shard_map.74), channel_id=1, source_target_pairs={{0,2},{8,10},{16,18},{24,26},{2,0},{10,8},{18,16},{26,24},{4,6},{1... | collective-permute-start | bytes 3686408 | tf_op jit(solution)/shard_map/ppermute | solution.py:558
  39.2 19.7 %collective-permute-start.11 = (bf16[6,2,64,128]{3,2,1,0:T(8,128)(2,1)S(1)}, bf16[6,2,64,128]{3,2,1,0:T(8,128)(2,1)S(1)}, u32[]{:S(2)}, u32[]{:S(2)}) collective-permute-start(bf16[6,2,64,128]{3,2,1,0:T(8,128)(2,1)S(1)} %get-tuple-element.55), channel_id=1, source_target_pairs={{2,28},{26,4},{4,26},{28,2},{3,29},{27,5},{5,27},{29,3}} | collective-permute-start | bytes 589832 | tf_op jit(solution)/shard_map/ppermute | solution.py:558
  42.9 16.0 %collective-permute-start.12 = (bf16[6,2,64,128]{3,2,1,0:T(8,128)(2,1)S(1)}, bf16[6,2,64,128]{3,2,1,0:T(8,128)(2,1)S(1)}, u32[]{:S(2)}, u32[]{:S(2)}) collective-permute-start(bf16[6,2,64,128]{3,2,1,0:T(8,128)(2,1)S(1)} %get-tuple-element.56), channel_id=1, source_target_pairs={{0,26},{24,2},{2,24},{26,0},{4,30},{28,6},{6,28},{30,4},{1,27},{25... | collective-permute-start | bytes 589832 | tf_op jit(solution)/shard_map/ppermute | solution.py:558
  45.0 15.1 %collective-permute-start.10 = (bf16[6,2,64,128]{3,2,1,0:T(8,128)(2,1)S(1)}, bf16[6,2,64,128]{3,2,1,0:T(8,128)(2,1)S(1)}, u32[]{:S(2)}, u32[]{:S(2)}) collective-permute-start(bf16[6,2,64,128]{3,2,1,0:T(8,128)(2,1)S(1)} %shard_map.78), channel_id=1, source_target_pairs={{0,18},{24,10},{18,26},{10,2},{2,16},{26,8},{16,24},{8,0},{4,22},{... | collective-permute-start | bytes 589832 | tf_op jit(solution)/shard_map/ppermute | solution.py:558
  45.8 14.4 %collective-permute-start.9 = (bf16[6,2,64,128]{3,2,1,0:T(8,128)(2,1)S(1)}, bf16[6,2,64,128]{3,2,1,0:T(8,128)(2,1)S(1)}, u32[]{:S(2)}, u32[]{:S(2)}) collective-permute-start(bf16[6,2,64,128]{3,2,1,0:T(8,128)(2,1)S(1)} %shard_map.77), channel_id=1, source_target_pairs={{2,20},{26,12},{20,28},{12,4},{4,18},{28,10},{18,26},{10,2},{3,21}... | collective-permute-start | bytes 589832 | tf_op jit(solution)/shard_map/ppermute | solution.py:558
where the time goes:
time: 66.9 us; the launch traced here: 66.4 us
  starting transfers between devices  36.9 us (55%)
  Pallas kernels  16.9 us (25%)
  local copies, waits for them, and re-layouts  5.2 us (8%)
  blocking collectives  3.79 us (6%)
  other arithmetic  2.39 us (4%)
  waiting for transfers between devices  0.79 us (1%)
    ppermute x11, starting transfers between devices, send(): return lax.ppermute(array, ('dp', 'pipe'), pairs)  29.6 us
    pallas_call x2, Pallas kernels, local_part(): pl.pallas_call(functools.partial(message_kernel, turn, group), grid_spec=...  6.91 us
    ppermute x1, starting transfers between devices, body_chain(): ids_3 = lax.ppermute(own_ids, 'dp', [(0, 3), (3, 0)])  6.06 us
    pallas_call x2, Pallas kernels, body_chain(): pl.pallas_call(near_kernel, out_shape=[wide, wide, wide, row, square, jax...  5.34 us
    psum x1, blocking collectives, body_chain(): total = lax.psum(jnp.sum(squares, axis=2), 'tensor')  3.79 us
    unnamed x14, local copies, waits for them, and re-layouts  3.71 us
    pallas_call x2, Pallas kernels, body_chain(): pl.pallas_call(functools.partial(tile_kernel, index, last), out_shape=pai...  2.39 us
    squeeze x1, local copies, waits for them, and re-layouts, body_chain(): lax.dynamic_index_in_dim(kv, c, 1, keepdims=False)  1.48 us
  transfers between devices with their start and end apart: 13, of which 2 were waited for; matrix products, arithmetic and copies ran while one was open for 4% of the time, Pallas kernels for 24%

commit v1 on v0

--- a/solution.py
+++ b/solution.py
@@ -608,8 +608,13 @@
     )(ids_3, *kvs)
     far_3 = [send(distant[turn], turn, [(0, 3, True), (3, 0, True)]) for turn in range(2)]
 
-    far_2 = []
-    for turn in range(2):
+    wide = jax.ShapeDtypeStruct((BLK, width), jnp.float32)
+    row = jax.ShapeDtypeStruct((BLK, width), jnp.bfloat16)
+    square = jax.ShapeDtypeStruct((BLK, HD), jnp.float32)
+    far_2, near, infos = [None, None], [None, None], [None, None]
+    for turn in (1, 0):
+        if turn == 0:
+            ups[0], near[1][4] = lax.optimization_barrier((ups[0], near[1][4]))
         array = pl.pallas_call(
             functools.partial(forward_kernel, turn),
             out_shape=tiles,
@@ -625,15 +630,7 @@
             ups[turn],
             downs[turn],
         )
-        far_2.append(send(array, turn, [(0, 2, True), (3, 1, True), (2, 3, False), (1, 0, False)]))
-
-    wide = jax.ShapeDtypeStruct((BLK, width), jnp.float32)
-    row = jax.ShapeDtypeStruct((BLK, width), jnp.bfloat16)
-    square = jax.ShapeDtypeStruct((BLK, HD), jnp.float32)
-    near, infos = [None, None], [None, None]
-    for turn in (1, 0):
-        if turn == 0:
-            messages[0], near[1][4] = lax.optimization_barrier((messages[0], near[1][4]))
+        far_2[turn] = send(array, turn, [(0, 2, True), (3, 1, True), (2, 3, False), (1, 0, False)])
         infos[turn] = messages[turn][0, width:].astype(jnp.int32)
         near[turn] = list(
             pl.pallas_call(

time: 66.9 us -> 68.7 us (1.027)
  the two profiles are of different devices: /device:TPU:1 before, /device:TPU:21 now
where the time goes in v1:
time: 68.7 us; the launch traced here: 68.3 us
  starting transfers between devices  28.3 us (41%)
  Pallas kernels  16.1 us (23%)
  waiting for transfers between devices  12.1 us (18%)
  local copies, waits for them, and re-layouts  5.2 us (8%)
  blocking collectives  3.8 us (6%)
  other arithmetic  2.37 us (3%)
    ppermute x11, starting transfers between devices, send(): return lax.ppermute(array, ('dp', 'pipe'), pairs)  25.7 us
    ppermute x11, waiting for transfers between devices, send(): return lax.ppermute(array, ('dp', 'pipe'), pairs)  12.1 us
    pallas_call x2, Pallas kernels, local_part(): pl.pallas_call(functools.partial(message_kernel, turn, group), grid_spec=...  6.91 us
    pallas_call x2, Pallas kernels, body_chain(): pl.pallas_call(near_kernel, out_shape=[wide, wide, wide, row, square, jax...  5.35 us
    psum x1, blocking collectives, body_chain(): total = lax.psum(jnp.sum(squares, axis=2), 'tensor')  3.8 us
    unnamed x14, local copies, waits for them, and re-layouts  3.71 us
    ppermute x1, starting transfers between devices, body_chain(): ids_2 = lax.ppermute(own_ids, 'dp', [(2, 0), (1, 3)])  1.95 us
    pallas_call x2, Pallas kernels, body_chain(): pl.pallas_call(functools.partial(tile_kernel, index, last), out_shape=pai...  1.81 us
  transfers between devices with their start and end apart: 13, of which 4 were waited for; matrix products, arithmetic and copies ran while one was open for 4% of the time, Pallas kernels for 22%

profile of v1, /device:TPU:21, one launch (start us, length us, event | category | flops | bytes accessed | tf_op | source)
XLA Modules:
  0.0 68.3 jit_solution(11560928405673284750)
XLA Ops:
  0.0 1.9 %collective-permute-start.1 = (s32[2,24]{1,0:T(2,128)}, s32[2,24]{1,0:T(2,128)S(1)}, u32[]{:S(2)}, u32[]{:S(2)}) collective-permute-start(s32[2,24]{1,0:T(2,128)} %bitcast.57), channel_id=1, source_target_pairs={{16,0},{8,24},{17,1},{9,25},{18,2},{10,26},{19,3},{11,27},{20,4},{... | collective-permute-start | bytes 584 | tf_op jit(solution)/shard_map/ppermute | solution.py:561
  3.3 1.5 %dynamic-slice_bitcast_fusion = (bf16[2,64,3072]{2,1,0:T(8,128)(2,1)S(1)}, bf16[2,64,3072]{2,1,0:T(8,128)(2,1)S(1)}) fusion(bf16[1,2,2,64,3072]{4,3,2,1,0:T(8,128)(2,1)} %param.9, s32[]{:T(128)S(6)} %select_n.11, s32[]{:T(128)S(6)} %select_n.10), kind=kLoop, calls=%fused_computation.4 | loop fusion | bytes 3145736 | tf_op jit(solution)/shard_map/jit(dynamic_index_in_dim)/squeeze | solution.py:567
  5.2 4.1 %collective-permute-start.2 = (bf16[2,64,3200]{2,1,0:T(8,128)(2,1)S(1)}, bf16[2,64,3200]{2,1,0:T(8,128)(2,1)S(1)}, u32[]{:S(2)}, u32[]{:S(2)}) collective-permute-start(bf16[2,64,3200]{2,1,0:T(8,128)(2,1)S(1)} %get-tuple-element.37.kv_ref.kv0_ref), channel_id=1, source_target_pairs={{2,4},{10,12},{18,20},{26,28},{4,2},{12,10},{20,18},{28,26},{3,5},... | collective-permute-start | bytes 2457608 | tf_op jit(solution)/shard_map/ppermute | solution.py:558
  9.3 1.9 %collective-permute-start.7 = (bf16[2,64,3200]{2,1,0:T(8,128)(2,1)S(1)}, bf16[2,64,3200]{2,1,0:T(8,128)(2,1)S(1)}, u32[]{:S(2)}, u32[]{:S(2)}) collective-permute-start(bf16[2,64,3200]{2,1,0:T(8,128)(2,1)S(1)} %get-tuple-element.42.kv_ref.kv1_ref), channel_id=1, source_target_pairs={{8,2},{16,10},{24,18},{10,0},{18,8},{26,16},{12,6},{20,14},{28,22}... | collective-permute-start | bytes 2457608 | tf_op jit(solution)/shard_map/ppermute | solution.py:558
  11.3 3.7 %collective-permute-start.6 = (bf16[2,64,3200]{2,1,0:T(8,128)(2,1)S(1)}, bf16[2,64,3200]{2,1,0:T(8,128)(2,1)S(1)}, u32[]{:S(2)}, u32[]{:S(2)}) collective-permute-start(bf16[2,64,3200]{2,1,0:T(8,128)(2,1)S(1)} %get-tuple-element.42.kv_ref.kv1_ref), channel_id=1, source_target_pairs={{0,10},{8,18},{16,26},{2,8},{10,16},{18,24},{4,14},{12,22},{20,30}... | collective-permute-start | bytes 2457608 | tf_op jit(solution)/shard_map/ppermute | solution.py:558
  15.1 3.7 %copy-done = bf16[1,2,2,384,3072]{4,3,2,1,0:T(8,128)(2,1)S(1)} copy-done((bf16[1,2,2,384,3072]{4,3,2,1,0:T(8,128)(2,1)S(1)}, bf16[1,2,2,384,3072]{4,3,2,1,0:T(8,128)(2,1)}, u32[]{:S(2)}) %copy-start) | copy-done | bytes 9437208
  18.7 3.5 %shard_map.73 = bf16[192,3200]{1,0:T(8,128)(2,1)S(1)} custom-call(s32[2]{0:T(128)S(1)} %pad_add_fusion.order_ref, s32[2,24]{1,0:T(2,128)S(1)} %bitcast.59, s32[2]{0:T(128)S(1)} %bitcast.61, bf16[2,64,3072]{2,1,0:T(8,128)(2,1)S(1)} %bitcast.53, bf16[2,64,3072]{2,1,0:T(8,128)(2,1)S(1)} %bitcast.55, bf16[2,2,64,3072]{3,2,1,0:T(8,128)(2,1)S(1)} %bitcast.51, ...), custom_call_target="tpu_custom_call" | custom-call | tf_op jit(solution)/shard_map/pallas_call | solution.py:580
  22.2 4.3 %collective-permute-start.8 = (bf16[2,64,3200]{2,1,0:T(8,128)(2,1)S(1)}, bf16[2,64,3200]{2,1,0:T(8,128)(2,1)S(1)}, u32[]{:S(2)}, u32[]{:S(2)}) collective-permute-start(bf16[2,64,3200]{2,1,0:T(8,128)(2,1)S(1)} %collective-permute-done.2), channel_id=1, source_target_pairs={{12,4},{20,12},{28,20},{10,2},{18,10},{26,18},{13,5},{21,13},{29,2... | collective-permute-start | bytes 2457608 | tf_op jit(solution)/shard_map/ppermute | solution.py:558
  26.5 3.5 %shard_map.74 = bf16[192,3200]{1,0:T(8,128)(2,1)S(1)} custom-call(s32[2]{0:T(128)S(1)} %pad_add_fusion.order_ref, s32[2,24]{1,0:T(2,128)S(1)} %bitcast.60, s32[2]{0:T(128)S(1)} %bitcast.62, bf16[2,64,3072]{2,1,0:T(8,128)(2,1)S(1)} %bitcast.54, bf16[2,64,3072]{2,1,0:T(8,128)(2,1)S(1)} %bitcast.56, bf16[2,2,64,3072]{3,2,1,0:T(8,128)(2,1)S(1)} %bitcast.52, ...), custom_call_target="tpu_custom_call" | custom-call | tf_op jit(solution)/shard_map/pallas_call | solution.py:580
  30.0 2.2 %collective-permute-start.3 = (bf16[192,3200]{1,0:T(8,128)(2,1)S(1)}, bf16[192,3200]{1,0:T(8,128)(2,1)S(1)}, u32[]{:S(2)}, u32[]{:S(2)}) collective-permute-start(bf16[192,3200]{1,0:T(8,128)(2,1)S(1)} %shard_map.73), channel_id=1, source_target_pairs={{2,4},{10,12},{18,20},{26,28},{4,2},{12,10},{20,18},{28,26},{3,5},... | collective-permute-start | bytes 3686408 | tf_op jit(solution)/shard_map/ppermute | solution.py:558
  32.9 2.2 %collective-permute-start.5 = (bf16[2,64,3200]{2,1,0:T(8,128)(2,1)S(1)}, bf16[2,64,3200]{2,1,0:T(8,128)(2,1)S(1)}, u32[]{:S(2)}, u32[]{:S(2)}) collective-permute-start(bf16[2,64,3200]{2,1,0:T(8,128)(2,1)S(1)} %collective-permute-done.2), channel_id=1, source_target_pairs={{4,12},{12,20},{20,28},{2,10},{10,18},{18,26},{5,13},{13,21},{21,2... | collective-permute-start | bytes 2457608 | tf_op jit(solution)/shard_map/ppermute | solution.py:558
  35.1 0.8 %collective-permute-done.6.up_ref = bf16[2,64,3200]{2,1,0:T(8,128)(2,1)S(1)} collective-permute-done((bf16[2,64,3200]{2,1,0:T(8,128)(2,1)S(1)}, bf16[2,64,3200]{2,1,0:T(8,128)(2,1)S(1)}, u32[]{:S(2)}, u32[]{:S(2)}) %collective-permute-start.6) | collective-permute-done | bytes 819232 | tf_op jit(solution)/shard_map/ppermute | solution.py:558
  36.5 0.7 %shard_map.78 = bf16[6,2,64,128]{3,2,1,0:T(8,128)(2,1)S(1)} custom-call(s32[2,24]{1,0:T(2,128)S(1)} %collective-permute-done.1.ids_ref, s32[128]{0:T(128)S(1)} %fusion.8.up_ids_ref, s32[128]{0:T(128)S(1)} %fusion.7.down_ids_ref, bf16[2,64,3200]{2,1,0:T(8,128)(2,1)S(1)} %get-tuple-element.42.kv_ref.kv1_ref, ...), custom_call_target="tpu_custom_call" | custom-call | tf_op jit(solution)/shard_map/pallas_call | solution.py:618
  37.3 3.3 %collective-permute-done.8.down_ref = bf16[2,64,3200]{2,1,0:T(8,128)(2,1)S(1)} collective-permute-done((bf16[2,64,3200]{2,1,0:T(8,128)(2,1)S(1)}, bf16[2,64,3200]{2,1,0:T(8,128)(2,1)S(1)}, u32[]{:S(2)}, u32[]{:S(2)}) %collective-permute-start.8) | collective-permute-done | bytes 819232 | tf_op jit(solution)/shard_map/ppermute | solution.py:558
  41.2 4.0 %collective-permute-start.10 = (bf16[6,2,64,128]{3,2,1,0:T(8,128)(2,1)S(1)}, bf16[6,2,64,128]{3,2,1,0:T(8,128)(2,1)S(1)}, u32[]{:S(2)}, u32[]{:S(2)}) collective-permute-start(bf16[6,2,64,128]{3,2,1,0:T(8,128)(2,1)S(1)} %shard_map.78), channel_id=1, source_target_pairs={{0,18},{24,10},{18,26},{10,2},{2,16},{26,8},{16,24},{8,0},{4,22},{... | collective-permute-start | bytes 589832 | tf_op jit(solution)/shard_map/ppermute | solution.py:558
  45.3 2.7 %shard_map.75 = (f32[64,3072]{1,0:T(8,128)S(1)}, f32[64,3072]{1,0:T(8,128)S(1)}, f32[64,3072]{1,0:T(8,128)S(1)}, bf16[64,3072]{1,0:T(8,128)(2,1)S(1)}, f32[64,128]{1,0:T(8,128)S(1)}, /*index=5*/s32[2,6]{1,0:T(2,128)S(1)}) custom-call(s32[128]{0:T(128)S(1)} %fusion.10.info_ref.refs_1_, bf16[192,3200]{1,0:T(8,128)(2,1)S(1)} %collective-permute-done.4.message_ref.refs_5_, ...), custom_call_target="tpu_custom_call" | custom-call | tf_op jit(solution)/shard_map/pallas_call | solution.py:636
  48.0 0.7 %shard_map.77 = bf16[6,2,64,128]{3,2,1,0:T(8,128)(2,1)S(1)} custom-call(s32[2,24]{1,0:T(2,128)S(1)} %collective-permute-done.1.ids_ref, s32[128]{0:T(128)S(1)} %bitcast_convert_fusion.1.up_ids_ref, s32[128]{0:T(128)S(1)} %fusion.9.down_ids_ref, bf16[2,64,3200]{2,1,0:T(8,128)(2,1)S(1)} %get-tuple-element.37.kv_ref.kv0_ref, ...), custom_call_target="tpu_custom_call" | custom-call | tf_op jit(solution)/shard_map/pallas_call | solution.py:618
  48.7 1.9 %collective-permute-start.9 = (bf16[6,2,64,128]{3,2,1,0:T(8,128)(2,1)S(1)}, bf16[6,2,64,128]{3,2,1,0:T(8,128)(2,1)S(1)}, u32[]{:S(2)}, u32[]{:S(2)}) collective-permute-start(bf16[6,2,64,128]{3,2,1,0:T(8,128)(2,1)S(1)} %shard_map.77), channel_id=1, source_target_pairs={{2,20},{26,12},{20,28},{12,4},{4,18},{28,10},{18,26},{10,2},{3,21}... | collective-permute-start | bytes 589832 | tf_op jit(solution)/shard_map/ppermute | solution.py:558
  50.7 2.7 %shard_map.76 = (f32[64,3072]{1,0:T(8,128)S(1)}, f32[64,3072]{1,0:T(8,128)S(1)}, f32[64,3072]{1,0:T(8,128)S(1)}, bf16[64,3072]{1,0:T(8,128)(2,1)S(1)}, f32[64,128]{1,0:T(8,128)S(1)}, /*index=5*/s32[2,6]{1,0:T(2,128)S(1)}) custom-call(s32[128]{0:T(128)S(1)} %fusion.11.info_ref.refs_0_, bf16[192,3200]{1,0:T(8,128)(2,1)S(1)} %collective-permute-done.3.message_ref.refs_4_, ...), custom_call_target="tpu_custom_call" | custom-call | tf_op jit(solution)/shard_map/pallas_call | solution.py:636
  54.0 3.5 %collective-permute-done.10.refs_7_ = bf16[6,2,64,128]{3,2,1,0:T(8,128)(2,1)S(1)} collective-permute-done((bf16[6,2,64,128]{3,2,1,0:T(8,128)(2,1)S(1)}, bf16[6,2,64,128]{3,2,1,0:T(8,128)(2,1)S(1)}, u32[]{:S(2)}, u32[]{:S(2)}) %collective-permute-start.10) | collective-permute-done | bytes 196640 | tf_op jit(solution)/shard_map/ppermute | solution.py:558
  57.5 4.5 %collective-permute-done.9.refs_6_ = bf16[6,2,64,128]{3,2,1,0:T(8,128)(2,1)S(1)} collective-permute-done((bf16[6,2,64,128]{3,2,1,0:T(8,128)(2,1)S(1)}, bf16[6,2,64,128]{3,2,1,0:T(8,128)(2,1)S(1)}, u32[]{:S(2)}, u32[]{:S(2)}) %collective-permute-start.9) | collective-permute-done | bytes 196640 | tf_op jit(solution)/shard_map/ppermute | solution.py:558
  62.0 1.2 %shard_map.81 = (bf16[2,64,3072]{2,1,0:T(8,128)(2,1)S(1)}, f32[2,64,128]{2,1,0:T(8,128)S(1)}) custom-call(s32[128]{0:T(128)S(1)} %fusion.11.info_ref.refs_0_, s32[128]{0:T(128)S(1)} %fusion.10.info_ref.refs_1_, s32[2,6]{1,0:T(2,128)S(1)} %get-tuple-element.45.refs_2_, s32[2,6]{1,0:T(2,128)S(1)} %get-tuple-element.46.refs_3_, ...), custom_call_target="tpu_custom_call" | custom-call | tf_op jit(solution)/shard_map/pallas_call | solution.py:647
  63.3 3.8 %psum.7 = f32[2,64]{1,0:T(2,128)S(1)} all-reduce(f32[2,64]{1,0:T(2,128)S(1)} %reduce_sum.9), channel_id=1, replica_groups=mesh['dp'=4,'pipe'=4,'tensor'=2] {'tensor'}, use_global_device_ids=true, to_apply=%region_1.2 | all-reduce | flops 128 | bytes 1024 | tf_op jit(solution)/shard_map/psum | solution.py:659
  67.1 1.1 %fusion = bf16[1,2,64,3072]{3,2,1,0:T(8,128)(2,1)} fusion(bf16[2,64,3072]{2,1,0:T(8,128)(2,1)S(1)} %get-tuple-element.65, f32[2,3072]{1,0:T(2,128)S(1)} %bitcast_convert_fusion, f32[2,64]{1,0:T(2,128)S(1)} %add_rsqrt_fusion), kind=kLoop, calls=%fused_computation.3 | loop fusion | flops 1572864 | bytes 1597952 | tf_op jit(solution)/shard_map/broadcast_in_dim | solution.py:662
  (42 shorter events, 4.5 us)
Async XLA Ops:
  0.0 5.2 %collective-permute-start.1 = (s32[2,24]{1,0:T(2,128)}, s32[2,24]{1,0:T(2,128)S(1)}, u32[]{:S(2)}, u32[]{:S(2)}) collective-permute-start(s32[2,24]{1,0:T(2,128)} %bitcast.57), channel_id=1, source_target_pairs={{16,0},{8,24},{17,1},{9,25},{18,2},{10,26},{19,3},{11,27},{20,4},{... | collective-permute-start | bytes 584 | tf_op jit(solution)/shard_map/ppermute | solution.py:561
  2.0 3.3 %collective-permute-start = (s32[2,24]{1,0:T(2,128)}, s32[2,24]{1,0:T(2,128)S(1)}, u32[]{:S(2)}, u32[]{:S(2)}) collective-permute-start(s32[2,24]{1,0:T(2,128)} %bitcast.58), channel_id=1, source_target_pairs={{0,24},{24,0},{1,25},{25,1},{2,26},{26,2},{3,27},{27,3},{4,28},{28... | collective-permute-start | bytes 584 | tf_op jit(solution)/shard_map/ppermute | solution.py:560
  4.8 10.2 %copy-start.1 = (bf16[1,2,2,64,3072]{4,3,2,1,0:T(8,128)(2,1)S(1)}, bf16[1,2,2,64,3072]{4,3,2,1,0:T(8,128)(2,1)}, u32[]{:S(2)}) copy-start(bf16[1,2,2,64,3072]{4,3,2,1,0:T(8,128)(2,1)} %param.9) | copy-start | bytes 4718596
  4.8 10.2 %copy-start.2 = (bf16[1,2,64,3072]{3,2,1,0:T(8,128)(2,1)S(1)}, bf16[1,2,64,3072]{3,2,1,0:T(8,128)(2,1)}, u32[]{:S(2)}) copy-start(bf16[1,2,64,3072]{3,2,1,0:T(8,128)(2,1)} %param.8) | copy-start | bytes 2359300
  4.8 10.2 %copy-start.3 = (bf16[1,2,64,3072]{3,2,1,0:T(8,128)(2,1)S(1)}, bf16[1,2,64,3072]{3,2,1,0:T(8,128)(2,1)}, u32[]{:S(2)}) copy-start(bf16[1,2,64,3072]{3,2,1,0:T(8,128)(2,1)} %param.7) | copy-start | bytes 2359300
  4.9 10.2 %copy-start.4 = (s32[1,2,1,24]{3,2,1,0:T(1,128)S(1)}, s32[1,2,1,24]{3,2,1,0:T(1,128)}, u32[]{:S(2)}) copy-start(s32[1,2,1,24]{3,2,1,0:T(1,128)} %param.11) | copy-start | bytes 580
  4.9 10.2 %copy-start.5 = (s32[1,2]{1,0:T(1,128)S(1)}, s32[1,2]{1,0:T(1,128)}, u32[]{:S(2)}) copy-start(s32[1,2]{1,0:T(1,128)} %param.12) | copy-start | bytes 28
  5.2 17.0 %collective-permute-start.2 = (bf16[2,64,3200]{2,1,0:T(8,128)(2,1)S(1)}, bf16[2,64,3200]{2,1,0:T(8,128)(2,1)S(1)}, u32[]{:S(2)}, u32[]{:S(2)}) collective-permute-start(bf16[2,64,3200]{2,1,0:T(8,128)(2,1)S(1)} %get-tuple-element.37.kv_ref.kv0_ref), channel_id=1, source_target_pairs={{2,4},{10,12},{18,20},{26,28},{4,2},{12,10},{20,18},{28,26},{3,5},... | collective-permute-start | bytes 2457608 | tf_op jit(solution)/shard_map/ppermute | solution.py:558
  9.3 23.6 %collective-permute-start.7 = (bf16[2,64,3200]{2,1,0:T(8,128)(2,1)S(1)}, bf16[2,64,3200]{2,1,0:T(8,128)(2,1)S(1)}, u32[]{:S(2)}, u32[]{:S(2)}) collective-permute-start(bf16[2,64,3200]{2,1,0:T(8,128)(2,1)S(1)} %get-tuple-element.42.kv_ref.kv1_ref), channel_id=1, source_target_pairs={{8,2},{16,10},{24,18},{10,0},{18,8},{26,16},{12,6},{20,14},{28,22}... | collective-permute-start | bytes 2457608 | tf_op jit(solution)/shard_map/ppermute | solution.py:558
  11.3 24.5 %collective-permute-start.6 = (bf16[2,64,3200]{2,1,0:T(8,128)(2,1)S(1)}, bf16[2,64,3200]{2,1,0:T(8,128)(2,1)S(1)}, u32[]{:S(2)}, u32[]{:S(2)}) collective-permute-start(bf16[2,64,3200]{2,1,0:T(8,128)(2,1)S(1)} %get-tuple-element.42.kv_ref.kv1_ref), channel_id=1, source_target_pairs={{0,10},{8,18},{16,26},{2,8},{10,16},{18,24},{4,14},{12,22},{20,30}... | collective-permute-start | bytes 2457608 | tf_op jit(solution)/shard_map/ppermute | solution.py:558
  15.1 3.7 %copy-start = (bf16[1,2,2,384,3072]{4,3,2,1,0:T(8,128)(2,1)S(1)}, bf16[1,2,2,384,3072]{4,3,2,1,0:T(8,128)(2,1)}, u32[]{:S(2)}) copy-start(bf16[1,2,2,384,3072]{4,3,2,1,0:T(8,128)(2,1)} %param.10) | copy-start | bytes 28311556
  22.2 10.1 %copy-start.6 = (bf16[1,2,3072]{2,1,0:T(2,128)(2,1)S(1)}, bf16[1,2,3072]{2,1,0:T(2,128)(2,1)}, u32[]{:S(2)}) copy-start(bf16[1,2,3072]{2,1,0:T(2,128)(2,1)} %param.13) | copy-start | bytes 36868
  22.2 18.3 %collective-permute-start.8 = (bf16[2,64,3200]{2,1,0:T(8,128)(2,1)S(1)}, bf16[2,64,3200]{2,1,0:T(8,128)(2,1)S(1)}, u32[]{:S(2)}, u32[]{:S(2)}) collective-permute-start(bf16[2,64,3200]{2,1,0:T(8,128)(2,1)S(1)} %collective-permute-done.2), channel_id=1, source_target_pairs={{12,4},{20,12},{28,20},{10,2},{18,10},{26,18},{13,5},{21,13},{29,2... | collective-permute-start | bytes 2457608 | tf_op jit(solution)/shard_map/ppermute | solution.py:558
  30.0 20.6 %collective-permute-start.3 = (bf16[192,3200]{1,0:T(8,128)(2,1)S(1)}, bf16[192,3200]{1,0:T(8,128)(2,1)S(1)}, u32[]{:S(2)}, u32[]{:S(2)}) collective-permute-start(bf16[192,3200]{1,0:T(8,128)(2,1)S(1)} %shard_map.73), channel_id=1, source_target_pairs={{2,4},{10,12},{18,20},{26,28},{4,2},{12,10},{20,18},{28,26},{3,5},... | collective-permute-start | bytes 3686408 | tf_op jit(solution)/shard_map/ppermute | solution.py:558
  32.2 9.0 %collective-permute-start.4 = (bf16[192,3200]{1,0:T(8,128)(2,1)S(1)}, bf16[192,3200]{1,0:T(8,128)(2,1)S(1)}, u32[]{:S(2)}, u32[]{:S(2)}) collective-permute-start(bf16[192,3200]{1,0:T(8,128)(2,1)S(1)} %shard_map.74), channel_id=1, source_target_pairs={{0,2},{8,10},{16,18},{24,26},{2,0},{10,8},{18,16},{26,24},{4,6},{1... | collective-permute-start | bytes 3686408 | tf_op jit(solution)/shard_map/ppermute | solution.py:558
  32.9 15.1 %collective-permute-start.5 = (bf16[2,64,3200]{2,1,0:T(8,128)(2,1)S(1)}, bf16[2,64,3200]{2,1,0:T(8,128)(2,1)S(1)}, u32[]{:S(2)}, u32[]{:S(2)}) collective-permute-start(bf16[2,64,3200]{2,1,0:T(8,128)(2,1)S(1)} %collective-permute-done.2), channel_id=1, source_target_pairs={{4,12},{12,20},{20,28},{2,10},{10,18},{18,26},{5,13},{13,21},{21,2... | collective-permute-start | bytes 2457608 | tf_op jit(solution)/shard_map/ppermute | solution.py:558
  35.9 17.5 %collective-permute-start.11 = (bf16[6,2,64,128]{3,2,1,0:T(8,128)(2,1)S(1)}, bf16[6,2,64,128]{3,2,1,0:T(8,128)(2,1)S(1)}, u32[]{:S(2)}, u32[]{:S(2)}) collective-permute-start(bf16[6,2,64,128]{3,2,1,0:T(8,128)(2,1)S(1)} %get-tuple-element.55), channel_id=1, source_target_pairs={{2,28},{26,4},{4,26},{28,2},{3,29},{27,5},{5,27},{29,3}} | collective-permute-start | bytes 589832 | tf_op jit(solution)/shard_map/ppermute | solution.py:558
  40.5 12.8 %collective-permute-start.12 = (bf16[6,2,64,128]{3,2,1,0:T(8,128)(2,1)S(1)}, bf16[6,2,64,128]{3,2,1,0:T(8,128)(2,1)S(1)}, u32[]{:S(2)}, u32[]{:S(2)}) collective-permute-start(bf16[6,2,64,128]{3,2,1,0:T(8,128)(2,1)S(1)} %get-tuple-element.56), channel_id=1, source_target_pairs={{0,26},{24,2},{2,24},{26,0},{4,30},{28,6},{6,28},{30,4},{1,27},{25... | collective-permute-start | bytes 589832 | tf_op jit(solution)/shard_map/ppermute | solution.py:558
  41.2 16.3 %collective-permute-start.10 = (bf16[6,2,64,128]{3,2,1,0:T(8,128)(2,1)S(1)}, bf16[6,2,64,128]{3,2,1,0:T(8,128)(2,1)S(1)}, u32[]{:S(2)}, u32[]{:S(2)}) collective-permute-start(bf16[6,2,64,128]{3,2,1,0:T(8,128)(2,1)S(1)} %shard_map.78), channel_id=1, source_target_pairs={{0,18},{24,10},{18,26},{10,2},{2,16},{26,8},{16,24},{8,0},{4,22},{... | collective-permute-start | bytes 589832 | tf_op jit(solution)/shard_map/ppermute | solution.py:558
  48.7 13.3 %collective-permute-start.9 = (bf16[6,2,64,128]{3,2,1,0:T(8,128)(2,1)S(1)}, bf16[6,2,64,128]{3,2,1,0:T(8,128)(2,1)S(1)}, u32[]{:S(2)}, u32[]{:S(2)}) collective-permute-start(bf16[6,2,64,128]{3,2,1,0:T(8,128)(2,1)S(1)} %shard_map.77), channel_id=1, source_target_pairs={{2,20},{26,12},{20,28},{12,4},{4,18},{28,10},{18,26},{10,2},{3,21}... | collective-permute-start | bytes 589832 | tf_op jit(solution)/shard_map/ppermute | solution.py:558
